TPU v7x, 512 devices: a whole 4x4x16 slice. The times are simulated.
512 devices in a mesh: tm: 32 (over x, z_lo), space: 16 (over y, z_hi, core).
Axes of the slice: x: 4, y: 4, z: 16 (z_hi: 2, z_lo: 8; z = z_hi * 8 + z_lo), core: 2. Of those that a mesh axis runs over, the one named last changes fastest.
Arguments:
- u_old: float32 [32, 5, 256, 16, 128], P('tm', None, 'space'), may hold values from -2.5 to 2.5
- u_init: float32 [256, 16, 128], P('space'), may hold values from -2.5 to 2.5
Outputs:
- u_new: float32 [32, 5, 256, 16, 128], P('tm', None, 'space')
All inputs are finite; a program needn't handle non-finite values.
Results may differ from a plain program's by a relative error of at most 0.0003.
Values sent between devices are 32-bit elements; how exact they have to be, the bound alone decides.
No kernel may reach another device: no remote copies, remote signals or barrier semaphores. Data moves between devices by JAX's collectives and lax.ppermute only.
A program may use at most 64 MiB of HBM per device.

v0:
```python
import math
import jax
import jax.numpy as jnp
from jax import lax
from jax.sharding import Mesh
from jax.sharding import PartitionSpec as P

SPACE = ("space_0", "space_1", "space_2")
step_length = 0.4
diffusion = 1.0
reaction = 1.0


def passed_along(value, axis, steps):
    count = lax.axis_size(axis)
    leading, last = (max(0, -steps), min(count, count - steps))
    return lax.ppermute(value, axis, [(source, source + steps) for source in range(leading, last)])


def padded_2(x, sides, width):
    for axis, dim in sides:
        count, length = (lax.axis_size(axis), x.shape[dim])
        up = [(i, (i + 1) % count) for i in range(count)]
        down = [(j, i) for i, j in up]
        last = lax.slice_in_dim(x, length - width, length, axis=dim)
        leading = lax.slice_in_dim(x, 0, width, axis=dim)
        before = lax.ppermute(last, axis, up)
        after = lax.ppermute(leading, axis, down)
        x = jnp.concatenate([before, x, after], axis=dim)
    return x


def split_up(x, dim, count):
    before, after = (x.shape[:dim], x.shape[dim + 1 :])
    return jnp.moveaxis(x.reshape(*before, count, -1, *after), dim, 0)


def laid_out(parts, dim):
    parts = jnp.moveaxis(parts, 0, dim)
    lengths = parts.shape
    return parts.reshape(*lengths[:dim], lengths[dim] * lengths[dim + 1], *lengths[dim + 2 :])


def turned_blocks(parts, axes, sequence):
    lengths = [lax.axis_size(a) for a in axes]
    parts = parts.reshape(*lengths, *parts.shape[1:])
    for k in sequence:
        parts = lax.all_to_all(parts, axes[k], split_axis=k, concat_axis=k, tiled=True)
    return parts.reshape(-1, *parts.shape[len(axes) :])


def core_and_chips(x, groups, sequence, split_dim, concat_dim):
    count = lax.axis_size(groups[0]) * lax.axis_size(groups[1])
    parts = split_up(x, split_dim, count)
    return laid_out(turned_blocks(parts, groups, sequence), concat_dim)


def copy_for_each(x, axis):
    copies = jnp.broadcast_to(x, (lax.axis_size(axis), *x.shape))
    return lax.all_to_all(copies, axis, split_axis=0, concat_axis=0, tiled=True)


def collected_together(x, axis):
    leaves = jax.tree.leaves(x)
    sequence = sorted(range(len(leaves)), key=lambda k: -leaves[k].size)
    width = (1, *leaves[sequence[0]].shape)[-1]
    lines = [
        jnp.pad(leaves[k].reshape(-1), (0, -leaves[k].size % width)).reshape(-1, width)
        for k in sequence
    ]
    both, at, found = (copy_for_each(jnp.concatenate(lines), axis), 0, {})
    for k, line in zip(sequence, lines):
        piece = both[:, at : at + len(line)].reshape(len(both), -1)
        found[k] = piece[:, : leaves[k].size].reshape(-1, *leaves[k].shape)
        at += len(line)
    numbers = iter(range(len(leaves)))
    return jax.tree.map(lambda _: found[next(numbers)], x)


def combined_pairwise(pieces, combine):
    while len(jax.tree.leaves(pieces)[0]) > 1:
        pieces = jax.vmap(combine)(
            *(jax.tree.map(lambda part: part[side::2], pieces) for side in (0, 1))
        )
    return jax.tree.map(lambda part: part[0], pieces)


def carried_in(x, axis, combine, identity):
    count, index = (lax.axis_size(axis), lax.axis_index(axis))
    passed = jnp.arange(count) < index

    def kept(part, zero, own):
        part = jnp.where(
            passed.reshape(-1, *(1 for _ in own.shape)), part, jnp.asarray(zero, own.dtype)
        )
        return part

    pieces = collected_together(x, axis)
    return combined_pairwise(jax.tree.map(kept, pieces, identity, x), combine)


def basis_coefficients(nodes, chosen):
    polynomial = [1.0]
    for other, point in enumerate(nodes):
        if other == chosen:
            continue
        divisor = nodes[chosen] - point
        widened = [0.0] * (len(polynomial) + 1)
        for power, value in enumerate(polynomial):
            widened[power + 1] += value / divisor
            widened[power] -= value * point / divisor
        polynomial = widened
    return polynomial


def basis_value(nodes, chosen, where):
    result = 1.0
    for other, point in enumerate(nodes):
        if other != chosen:
            result *= (where - point) / (nodes[chosen] - point)
    return result


def node_tables():
    root = math.sqrt(3.0 / 7.0)
    fine_tau = [0.0, (1.0 - root) / 2.0, 0.5, (1.0 + root) / 2.0, 1.0]
    coarse_tau = [0.0, 0.5, 1.0]
    integ = []
    for j in range(4):
        row_values = []
        for k in range(5):
            polynomial = basis_coefficients(fine_tau, k)
            total = 0.0
            for power, value in enumerate(polynomial):
                total += (
                    value
                    * (fine_tau[j + 1] ** (power + 1) - fine_tau[j] ** (power + 1))
                    / (power + 1)
                )
            row_values.append(total)
        integ.append(row_values)
    interp = [[basis_value(coarse_tau, c, fine_tau[m]) for c in range(3)] for m in range(5)]
    spacing = [float(fine_tau[j + 1] - fine_tau[j]) for j in range(4)]
    return (jnp.asarray(integ, jnp.float32), spacing, jnp.asarray(interp, jnp.float32))


def hartley(length):
    counter = jnp.arange(length, dtype=jnp.int32)
    product = counter[:, None] * counter[None, :] % length
    phase = 2.0 * jnp.pi * product.astype(jnp.float32) / length
    return (jnp.cos(phase) + jnp.sin(phase)) / math.sqrt(length)


def local_force(padded):
    field = padded[:, 1:-1]
    near = padded[:, 2:] + padded[:, :-2] + jnp.roll(field, 1, 2) + jnp.roll(field, -1, 2)
    near = near + jnp.roll(field, 1, 3) + jnp.roll(field, -1, 3)
    return diffusion * (near - 6.0 * field) + reaction * (field - field * field * field)


def inner_planes(field, margin):
    return field[margin : field.shape[0] - margin]


def restrict(field):
    depth, rows, cols = field.shape
    return (
        field.reshape(depth // 2, 2, rows // 2, 2, cols // 2, 2)
        .mean(axis=(1, 3, 5))
        .reshape(depth // 2, rows * cols // 4)
    )


def compose(earlier, later):
    return (later[0] * earlier[0], later[0] * earlier[1] + later[1])


def shards(u_old, u_init):
    integ, spacing, interp = node_tables()
    highest = lax.Precision.HIGHEST
    depth, rows, cols = u_init.shape
    fine_old = u_old[0]
    previous = passed_along(fine_old[4], "tm", 1)
    position = lax.axis_index("tm")
    start = jnp.where(position == 0, u_init, previous)
    states = [start]
    forces = []
    together = jnp.concatenate([start[None], fine_old], 0)
    wide = padded_2(together, ((SPACE, 1),), 5)
    fold_wide = local_force(wide[1:])
    iold_wide = step_length * jnp.einsum("jk,kzxy->jzxy", integ, fold_wide, precision=highest)
    current = wide[0]
    for section in range(4):
        force_now = local_force(current[None])[0]
        forces.append(inner_planes(force_now, 4 - section))
        following = (
            inner_planes(current, 1)
            + step_length
            * spacing[section]
            * (force_now - inner_planes(fold_wide[section], section))
            + inner_planes(iold_wide[section], section)
        )
        states.append(inner_planes(following, 4 - section))
        current = following
    forces.append(local_force(current[None])[0])
    inew = step_length * jnp.einsum("jk,kzxy->jzxy", integ, jnp.stack(forces), precision=highest)
    stacked = jnp.stack(
        [
            restrict(states[0]),
            restrict(states[2]),
            restrict(states[4]),
            restrict(inew[0] + inew[1]),
            restrict(inew[2] + inew[3]),
            restrict(u_init),
        ]
    )
    planes_c = depth // 2
    rows_c = rows // 2
    cols_c = cols // 2
    depth_c = planes_c * lax.axis_size(SPACE)
    table_xy = jnp.kron(hartley(rows_c), hartley(cols_c))
    table_z = hartley(depth_c)
    spectral_xy = jnp.einsum("fzc,cd->fzd", stacked, table_xy, precision=highest)
    wave_z = jnp.arange(depth_c, dtype=jnp.int32)
    wave_xy = jnp.arange(rows_c * cols_c, dtype=jnp.int32)
    angle_z = 2.0 * jnp.cos(2.0 * jnp.pi * wave_z.astype(jnp.float32) / depth_c)
    angle_x = 2.0 * jnp.cos(2.0 * jnp.pi * (wave_xy // cols_c).astype(jnp.float32) / rows_c)
    angle_y = 2.0 * jnp.cos(2.0 * jnp.pi * (wave_xy % cols_c).astype(jnp.float32) / cols_c)
    eigen_all = 0.25 * (angle_z[:, None] + angle_x[None, :] + angle_y[None, :] - 6.0)
    place = lax.axis_index(SPACE)
    columns = core_and_chips(spectral_xy, (("space_0", "space_1"), "space_2"), (1, 0), 2, 1)
    spectra = jnp.einsum("qz,fzc->fqc", table_z, columns, precision=highest)
    width = columns.shape[2]
    eigen = lax.dynamic_slice_in_dim(eigen_all, place * width, width, 1)
    pieces = [spectra[k] for k in range(6)]
    damping = 0.5 * step_length * diffusion * eigen
    denom = 1.0 - damping
    lifted0 = pieces[3] - damping * pieces[1]
    lifted1 = pieces[4] - damping * pieces[2]
    slope = 1.0 / (denom * denom)
    offset = (lifted0 / denom + lifted1) / denom
    before_slope, before_offset = carried_in(
        (slope, offset), "tm", compose, (jnp.ones_like(slope), jnp.zeros_like(offset))
    )
    begin = before_slope * pieces[5] + before_offset
    middle = (begin + lifted0) / denom
    finish = (middle + lifted1) / denom
    delta = jnp.stack([begin - pieces[0], middle - pieces[1], finish - pieces[2]])
    planar = jnp.einsum("zq,fqc->fzc", table_z, delta, precision=highest)
    returned = lax.all_to_all(planar, SPACE, split_axis=1, concat_axis=2, tiled=True)
    real_space = jnp.einsum("fzc,cd->fzd", returned, table_xy, precision=highest)
    coarse_grid = real_space.reshape(3, planes_c, rows_c, cols_c)
    timed = jnp.einsum("mc,czxy->mzxy", interp, coarse_grid, precision=highest)
    upper = jnp.repeat(jnp.repeat(jnp.repeat(timed, 2, 1), 2, 2), 2, 3)
    return (jnp.stack(states) + upper)[None]


def solution(mesh):
    finer = Mesh(
        mesh.devices.reshape(mesh.shape["tm"], 4, 2, 2), ("tm", "space_0", "space_1", "space_2")
    )
    in_specs = (P("tm", None, SPACE, None, None), P(SPACE, None, None))
    out_specs = P("tm", None, SPACE, None, None)
    return jax.shard_map(
        shards, mesh=finer, in_specs=in_specs, out_specs=out_specs, check_vma=False
    )
```

profile of v0, /device:TPU:1, one launch (start us, length us, event | category | flops | bytes accessed | tf_op | source)
XLA Modules:
  0.0 267.7 jit_solution(8408288563641661195)
XLA Ops:
  0.9 4.4 %collective-permute-start = (f32[16,16,128]{2,1,0:T(8,128)S(1)}, f32[16,16,128]{2,1,0:T(8,128)S(1)}, u32[]{:S(2)}, u32[]{:S(2)}) collective-permute-start(f32[16,16,128]{2,1,0:T(8,128)S(1)} %slice_bitcast_fusion.2), channel_id=1, source_target_pairs={{0,16},{16,32},{32,48},{48,64},{64,80},{80,96},{96,112},{112,128},... | collective-permute-start | bytes 393224 | tf_op jit(solution)/shard_map/ppermute | solution.py:17
  5.5 10.5 %reshape.343 = f32[8,2,8,2,64,2]{5,4,3,2,1,0:T(8,128)} reshape(f32[16,16,128]{2,1,0:T(8,128)} %param.5) | data formatting | bytes 262144 | tf_op jit(solution)/shard_map/reshape | solution.py:168
  16.0 4.0 %reduce_sum.59 = f32[8,8,64]{2,1,0:T(8,128)S(1)} reduce(f32[8,2,8,2,64,2]{5,4,3,2,1,0:T(8,128)} %reshape.343, f32[]{:T(128)} %constant.162.clone.1), dimensions={1,3,5}, to_apply=%region_5.6 | reduce | flops 28672 | bytes 147460 | tf_op jit(solution)/shard_map/reduce_sum | solution.py:169
  24.3 9.7 %reshape.340 = f32[8,2,8,2,64,2]{5,4,3,2,1,0:T(8,128)} reshape(f32[16,16,128]{2,1,0:T(8,128)S(1)} %get-tuple-element.20) | data formatting | bytes 262144 | tf_op jit(solution)/shard_map/reshape | solution.py:168
  34.1 15.4 %collective-permute-start.1 = (f32[6,5,16,128]{3,2,1,0:T(8,128)S(1)}, f32[6,5,16,128]{3,2,1,0:T(8,128)S(1)}, u32[]{:S(2)}, u32[]{:S(2)}) collective-permute-start(f32[6,5,16,128]{3,2,1,0:T(8,128)S(1)} %get-tuple-element.35), channel_id=1, source_target_pairs={{0,1},{1,2},{2,3},{3,4},{4,5},{5,6},{6,7},{7,8},{8,9},{9,10},{10,1... | collective-permute-start | bytes 737288 | tf_op jit(solution)/shard_map/ppermute | solution.py:27
  51.6 4.0 %reduce_sum.54 = f32[8,8,64]{2,1,0:T(8,128)S(1)} reduce(f32[8,2,8,2,64,2]{5,4,3,2,1,0:T(8,128)} %reshape.340, f32[]{:T(128)} %constant.162.clone.1), dimensions={1,3,5}, to_apply=%region_0.1 | reduce | flops 28672 | bytes 147460 | tf_op jit(solution)/shard_map/reduce_sum | solution.py:169
  55.7 13.5 %collective-permute-done.1 = f32[6,5,16,128]{3,2,1,0:T(8,128)S(1)} collective-permute-done((f32[6,5,16,128]{3,2,1,0:T(8,128)S(1)}, f32[6,5,16,128]{3,2,1,0:T(8,128)S(1)}, u32[]{:S(2)}, u32[]{:S(2)}) %collective-permute-start.1) | collective-permute-done | bytes 245792 | tf_op jit(solution)/shard_map/ppermute | solution.py:27
  69.2 7.4 %collective-permute-done.2 = f32[6,5,16,128]{3,2,1,0:T(8,128)S(1)} collective-permute-done((f32[6,5,16,128]{3,2,1,0:T(8,128)S(1)}, f32[6,5,16,128]{3,2,1,0:T(8,128)S(1)}, u32[]{:S(2)}, u32[]{:S(2)}) %collective-permute-start.2) | collective-permute-done | bytes 245792 | tf_op jit(solution)/shard_map/ppermute | solution.py:28
  85.1 10.0 %add.346 = f32[8,2,8,2,64,2]{5,4,3,2,1,0:T(8,128)} reshape(f32[16,16,128]{2,1,0:T(8,128)S(1)} %get-tuple-element.6) | data formatting | bytes 262144 | tf_op jit(solution)/shard_map/add | solution.py:212
  95.1 4.0 %reduce_sum.57 = f32[8,8,64]{2,1,0:T(8,128)S(1)} reduce(f32[8,2,8,2,64,2]{5,4,3,2,1,0:T(8,128)} %add.346, f32[]{:T(128)} %constant.162.clone.1), dimensions={1,3,5}, to_apply=%region_3.4 | reduce | flops 28672 | bytes 147460 | tf_op jit(solution)/shard_map/reduce_sum | solution.py:169
  99.2 9.7 %reshape.342 = f32[8,2,8,2,64,2]{5,4,3,2,1,0:T(8,128)} reshape(f32[1,16,16,128]{3,2,1,0:T(8,128)S(1)} %get-tuple-element.66) | data formatting | bytes 262144 | tf_op jit(solution)/shard_map/reshape | solution.py:168
  109.0 4.0 %reduce_sum.56 = f32[8,8,64]{2,1,0:T(8,128)S(1)} reduce(f32[8,2,8,2,64,2]{5,4,3,2,1,0:T(8,128)} %reshape.342, f32[]{:T(128)} %constant.162.clone.1), dimensions={1,3,5}, to_apply=%region_2.3 | reduce | flops 28672 | bytes 147460 | tf_op jit(solution)/shard_map/reduce_sum | solution.py:169
  113.1 9.7 %reshape.341 = f32[8,2,8,2,64,2]{5,4,3,2,1,0:T(8,128)} reshape(f32[1,16,16,128]{3,2,1,0:T(8,128)S(1)} %slice.664) | data formatting | bytes 262144 | tf_op jit(solution)/shard_map/reshape | solution.py:168
  122.8 4.0 %reduce_sum.55 = f32[8,8,64]{2,1,0:T(8,128)S(1)} reduce(f32[8,2,8,2,64,2]{5,4,3,2,1,0:T(8,128)} %reshape.341, f32[]{:T(128)} %constant.162.clone.1), dimensions={1,3,5}, to_apply=%region_1.2 | reduce | flops 28672 | bytes 147460 | tf_op jit(solution)/shard_map/reduce_sum | solution.py:169
  126.9 9.7 %add.348 = f32[8,2,8,2,64,2]{5,4,3,2,1,0:T(8,128)} reshape(f32[16,16,128]{2,1,0:T(8,128)S(1)} %get-tuple-element.5) | data formatting | bytes 262144 | tf_op jit(solution)/shard_map/add | solution.py:213
  136.6 4.0 %reduce_sum.58 = f32[8,8,64]{2,1,0:T(8,128)S(1)} reduce(f32[8,2,8,2,64,2]{5,4,3,2,1,0:T(8,128)} %add.348, f32[]{:T(128)} %constant.162.clone.1), dimensions={1,3,5}, to_apply=%region_4.5 | reduce | flops 28672 | bytes 147460 | tf_op jit(solution)/shard_map/reduce_sum | solution.py:169
  143.6 3.5 %all_to_all.33 = f32[2,1,12288]{2,1,0:T(1,128)S(1)} all-to-all(f32[2,1,12288]{2,1,0:T(1,128)S(1)} %reshape.389), channel_id=1, replica_groups=mesh['tm'=32,'space_0'=4,'space_1'=2,'space_2'=2] {'space_2'}, dimensions={0} | all-to-all | bytes 196608 | tf_op jit(solution)/shard_map/all_to_all | solution.py:48
  149.6 8.5 %all-to-all-start.1 = ((f32[8,1,3072]{2,1,0:T(1,128)}), f32[8,1,3072]{2,1,0:T(1,128)S(1)}, u32[]{:S(2)}, u32[]{:S(2)}) async-start(f32[8,1,3072]{2,1,0:T(1,128)} %reshape.391), calls=%async_computation.1 | async-start | bytes 196608 | tf_op jit(solution)/shard_map/all_to_all | solution.py:48
  158.4 13.8 %all-to-all-done.1 = f32[8,1,3072]{2,1,0:T(1,128)S(1)} async-done(((f32[8,1,3072]{2,1,0:T(1,128)}), f32[8,1,3072]{2,1,0:T(1,128)S(1)}, u32[]{:S(2)}, u32[]{:S(2)}) %all-to-all-start.1) | async-done | bytes 98336 | tf_op jit(solution)/shard_map/all_to_all | solution.py:48
  175.3 7.4 %all-to-all-start.2 = ((f32[32,256,32]{1,2,0:T(8,128)}), f32[32,256,32]{1,2,0:T(8,128)S(1)}, u32[]{:S(2)}, u32[]{:S(2)}) async-start(f32[32,256,32]{1,2,0:T(8,128)} %broadcast_in_dim.60), calls=%async_computation.2 | async-start | bytes 2097152 | tf_op jit(solution)/shard_map/all_to_all | solution.py:60
  184.7 48.1 %all-to-all-done.2 = f32[32,256,32]{1,2,0:T(8,128)S(1)} async-done(((f32[32,256,32]{1,2,0:T(8,128)}), f32[32,256,32]{1,2,0:T(8,128)S(1)}, u32[]{:S(2)}, u32[]{:S(2)}) %all-to-all-start.2) | async-done | bytes 1048608 | tf_op jit(solution)/shard_map/all_to_all | solution.py:60
  234.8 7.0 %all-to-all-start.3 = ((f32[16,1,768]{2,1,0:T(1,128)}), f32[16,1,768]{2,1,0:T(1,128)S(1)}, u32[]{:S(2)}, u32[]{:S(2)}) async-start(f32[16,1,768]{2,1,0:T(1,128)} %reshape.393), calls=%async_computation.3 | async-start | bytes 98304 | tf_op jit(solution)/shard_map/all_to_all | solution.py:250
  242.6 13.9 %all-to-all-done.3 = f32[16,1,768]{2,1,0:T(1,128)S(1)} async-done(((f32[16,1,768]{2,1,0:T(1,128)}), f32[16,1,768]{2,1,0:T(1,128)S(1)}, u32[]{:S(2)}, u32[]{:S(2)}) %all-to-all-start.3) | async-done | bytes 49184 | tf_op jit(solution)/shard_map/all_to_all | solution.py:250
  263.5 3.3 %copy.110 = f32[1,5,16,16,128]{4,3,2,1,0:T(8,128)S(1)} copy(f32[1,5,16,16,128]{3,2,4,1,0:T(8,128)} %bitcast.144) | data formatting | bytes 1310720 | tf_op jit(solution)/shard_map/reshape | solution.py:254
  (124 shorter events, 37.4 us)
Async XLA Ops:
  0.9 22.7 %collective-permute-start = (f32[16,16,128]{2,1,0:T(8,128)S(1)}, f32[16,16,128]{2,1,0:T(8,128)S(1)}, u32[]{:S(2)}, u32[]{:S(2)}) collective-permute-start(f32[16,16,128]{2,1,0:T(8,128)S(1)} %slice_bitcast_fusion.2), channel_id=1, source_target_pairs={{0,16},{16,32},{32,48},{48,64},{64,80},{80,96},{96,112},{112,128},... | collective-permute-start | bytes 393224 | tf_op jit(solution)/shard_map/ppermute | solution.py:17
  21.7 2.0 copy-start.2
  24.3 9.7 %copy-start = (f32[1,5,16,16,128]{4,3,2,1,0:T(8,128)S(1)}, f32[1,5,16,16,128]{4,3,2,1,0:T(8,128)}, u32[]{:S(2)}) copy-start(f32[1,5,16,16,128]{4,3,2,1,0:T(8,128)} %param.4) | copy-start | bytes 1966084
  34.1 35.1 %collective-permute-start.1 = (f32[6,5,16,128]{3,2,1,0:T(8,128)S(1)}, f32[6,5,16,128]{3,2,1,0:T(8,128)S(1)}, u32[]{:S(2)}, u32[]{:S(2)}) collective-permute-start(f32[6,5,16,128]{3,2,1,0:T(8,128)S(1)} %get-tuple-element.35), channel_id=1, source_target_pairs={{0,1},{1,2},{2,3},{3,4},{4,5},{5,6},{6,7},{7,8},{8,9},{9,10},{10,1... | collective-permute-start | bytes 737288 | tf_op jit(solution)/shard_map/ppermute | solution.py:27
  49.5 27.1 %collective-permute-start.2 = (f32[6,5,16,128]{3,2,1,0:T(8,128)S(1)}, f32[6,5,16,128]{3,2,1,0:T(8,128)S(1)}, u32[]{:S(2)}, u32[]{:S(2)}) collective-permute-start(f32[6,5,16,128]{3,2,1,0:T(8,128)S(1)} %get-tuple-element.36), channel_id=1, source_target_pairs={{1,0},{2,1},{3,2},{4,3},{5,4},{6,5},{7,6},{8,7},{9,8},{10,9},{11,1... | collective-permute-start | bytes 737288 | tf_op jit(solution)/shard_map/ppermute | solution.py:28
  77.8 0.9 copy-start.3
  149.6 22.6 %all-to-all-start.1 = ((f32[8,1,3072]{2,1,0:T(1,128)}), f32[8,1,3072]{2,1,0:T(1,128)S(1)}, u32[]{:S(2)}, u32[]{:S(2)}) async-start(f32[8,1,3072]{2,1,0:T(1,128)} %reshape.391), calls=%async_computation.1 | async-start | bytes 196608 | tf_op jit(solution)/shard_map/all_to_all | solution.py:48
  175.3 57.5 %all-to-all-start.2 = ((f32[32,256,32]{1,2,0:T(8,128)}), f32[32,256,32]{1,2,0:T(8,128)S(1)}, u32[]{:S(2)}, u32[]{:S(2)}) async-start(f32[32,256,32]{1,2,0:T(8,128)} %broadcast_in_dim.60), calls=%async_computation.2 | async-start | bytes 2097152 | tf_op jit(solution)/shard_map/all_to_all | solution.py:60
  234.8 21.6 %all-to-all-start.3 = ((f32[16,1,768]{2,1,0:T(1,128)}), f32[16,1,768]{2,1,0:T(1,128)S(1)}, u32[]{:S(2)}, u32[]{:S(2)}) async-start(f32[16,1,768]{2,1,0:T(1,128)} %reshape.393), calls=%async_computation.3 | async-start | bytes 98304 | tf_op jit(solution)/shard_map/all_to_all | solution.py:250
  257.2 1.8 copy-start.4
  263.5 3.3 %copy-start.1 = (f32[1,5,16,16,128]{4,3,2,1,0:T(8,128)S(1)}, f32[1,5,16,16,128]{4,3,2,1,0:T(8,128)}, u32[]{:S(2)}) copy-start(f32[1,5,16,16,128]{4,3,2,1,0:T(8,128)} %bitcast_dynamic-update-slice_fusion) | copy-start | bytes 1966084
where the time goes:
time: 269 us; the launch traced here: 268 us
  waiting for transfers between devices  96.6 us (36%)
  local copies, waits for them, and re-layouts  79.5 us (30%)
  starting transfers between devices  44.8 us (17%)
  other arithmetic  33.6 us (12%)
  matrix products  9.05 us (3%)
  blocking collectives  3.45 us (1%)
    all_to_all x1, waiting for transfers between devices, copy_for_each(): return lax.all_to_all(copies, axis, split_axis=0, concat_axis=0, tiled=True)  48.1 us
    reshape x4, local copies, waits for them, and re-layouts, restrict(): field.reshape(depth // 2, 2, rows // 2, 2, cols // 2, 2)  39.7 us
    reduce_sum x6, other arithmetic, restrict(): return field.reshape(depth // 2, 2, rows // 2, 2, cols // 2, 2).mean(axis...  24.1 us
    ppermute x1, starting transfers between devices, padded_2(): before = lax.ppermute(last, axis, up)  15.4 us
    all_to_all x1, waiting for transfers between devices, shards(): lax.all_to_all(planar, SPACE, split_axis=1, concat_axis=2, tiled=True)  13.9 us
    all_to_all x1, waiting for transfers between devices, turned_blocks(): lax.all_to_all(parts, axes[k], split_axis=k, concat_axis=k, tiled=True)  13.8 us
    ppermute x1, waiting for transfers between devices, padded_2(): before = lax.ppermute(last, axis, up)  13.5 us
    add x1, local copies, waits for them, and re-layouts, shards(): inew[0] + inew[1]  9.98 us
  transfers between devices with their start and end apart: 6, of which 5 were waited for; matrix products, arithmetic and copies ran while one was open for 9% of the time, Pallas kernels for 0%

commit v1 on v0

--- a/solution.py
+++ b/solution.py
@@ -247,7 +247,10 @@
     finish = (middle + lifted1) / denom
     delta = jnp.stack([begin - pieces[0], middle - pieces[1], finish - pieces[2]])
     planar = jnp.einsum("zq,fqc->fzc", table_z, delta, precision=highest)
-    returned = lax.all_to_all(planar, SPACE, split_axis=1, concat_axis=2, tiled=True)
+    count_2 = lax.axis_size(SPACE)
+    blocks = jnp.stack(jnp.split(planar, count_2, axis=1), axis=0)
+    blocks = lax.all_to_all(blocks, SPACE, split_axis=0, concat_axis=0)
+    returned = jnp.concatenate(blocks, axis=2)
     real_space = jnp.einsum("fzc,cd->fzd", returned, table_xy, precision=highest)
     coarse_grid = real_space.reshape(3, planes_c, rows_c, cols_c)
     timed = jnp.einsum("mc,czxy->mzxy", interp, coarse_grid, precision=highest)

time: 269 us -> 270 us (level)
  no operation moved by 1% of the time
where the time goes in v1:
time: 270 us; the launch traced here: 269 us
  waiting for transfers between devices  96.6 us (36%)
  local copies, waits for them, and re-layouts  80.8 us (30%)
  starting transfers between devices  44.9 us (17%)
  other arithmetic  33.6 us (12%)
  matrix products  9.05 us (3%)
  blocking collectives  3.45 us (1%)
    all_to_all x1, waiting for transfers between devices, copy_for_each(): return lax.all_to_all(copies, axis, split_axis=0, concat_axis=0, tiled=True)  48.1 us
    reshape x4, local copies, waits for them, and re-layouts, restrict(): field.reshape(depth // 2, 2, rows // 2, 2, cols // 2, 2)  39.7 us
    reduce_sum x6, other arithmetic, restrict(): return field.reshape(depth // 2, 2, rows // 2, 2, cols // 2, 2).mean(axis...  24.1 us
    ppermute x1, starting transfers between devices, padded_2(): before = lax.ppermute(last, axis, up)  15.4 us
    all_to_all x1, waiting for transfers between devices, shards(): blocks = lax.all_to_all(blocks, SPACE, split_axis=0, concat_axis=0)  13.9 us
    all_to_all x1, waiting for transfers between devices, turned_blocks(): lax.all_to_all(parts, axes[k], split_axis=k, concat_axis=k, tiled=True)  13.8 us
    ppermute x1, waiting for transfers between devices, padded_2(): before = lax.ppermute(last, axis, up)  13.5 us
    add x1, local copies, waits for them, and re-layouts, shards(): inew[0] + inew[1]  9.97 us
  transfers between devices with their start and end apart: 6, of which 5 were waited for; matrix products, arithmetic and copies ran while one was open for 9% of the time, Pallas kernels for 0%

profile of v1, /device:TPU:1, one launch (start us, length us, event | category | flops | bytes accessed | tf_op | source)
XLA Modules:
  0.0 269.2 jit_solution(9572170724353152795)
XLA Ops:
  0.9 4.4 %collective-permute-start = (f32[16,16,128]{2,1,0:T(8,128)S(1)}, f32[16,16,128]{2,1,0:T(8,128)S(1)}, u32[]{:S(2)}, u32[]{:S(2)}) collective-permute-start(f32[16,16,128]{2,1,0:T(8,128)S(1)} %slice_bitcast_fusion.2), channel_id=1, source_target_pairs={{0,16},{16,32},{32,48},{48,64},{64,80},{80,96},{96,112},{112,128},... | collective-permute-start | bytes 393224 | tf_op jit(solution)/shard_map/ppermute | solution.py:17
  5.5 10.5 %reshape.349 = f32[8,2,8,2,64,2]{5,4,3,2,1,0:T(8,128)} reshape(f32[16,16,128]{2,1,0:T(8,128)} %param.5) | data formatting | bytes 262144 | tf_op jit(solution)/shard_map/reshape | solution.py:168
  16.0 4.0 %reduce_sum.59 = f32[8,8,64]{2,1,0:T(8,128)S(1)} reduce(f32[8,2,8,2,64,2]{5,4,3,2,1,0:T(8,128)} %reshape.349, f32[]{:T(128)} %constant.162.clone.1), dimensions={1,3,5}, to_apply=%region_5.6 | reduce | flops 28672 | bytes 147460 | tf_op jit(solution)/shard_map/reduce_sum | solution.py:169
  24.3 9.7 %reshape.346 = f32[8,2,8,2,64,2]{5,4,3,2,1,0:T(8,128)} reshape(f32[16,16,128]{2,1,0:T(8,128)S(1)} %get-tuple-element.20) | data formatting | bytes 262144 | tf_op jit(solution)/shard_map/reshape | solution.py:168
  34.1 15.4 %collective-permute-start.1 = (f32[6,5,16,128]{3,2,1,0:T(8,128)S(1)}, f32[6,5,16,128]{3,2,1,0:T(8,128)S(1)}, u32[]{:S(2)}, u32[]{:S(2)}) collective-permute-start(f32[6,5,16,128]{3,2,1,0:T(8,128)S(1)} %get-tuple-element.35), channel_id=1, source_target_pairs={{0,1},{1,2},{2,3},{3,4},{4,5},{5,6},{6,7},{7,8},{8,9},{9,10},{10,1... | collective-permute-start | bytes 737288 | tf_op jit(solution)/shard_map/ppermute | solution.py:27
  51.6 4.0 %reduce_sum.54 = f32[8,8,64]{2,1,0:T(8,128)S(1)} reduce(f32[8,2,8,2,64,2]{5,4,3,2,1,0:T(8,128)} %reshape.346, f32[]{:T(128)} %constant.162.clone.1), dimensions={1,3,5}, to_apply=%region_0.1 | reduce | flops 28672 | bytes 147460 | tf_op jit(solution)/shard_map/reduce_sum | solution.py:169
  55.7 13.5 %collective-permute-done.1 = f32[6,5,16,128]{3,2,1,0:T(8,128)S(1)} collective-permute-done((f32[6,5,16,128]{3,2,1,0:T(8,128)S(1)}, f32[6,5,16,128]{3,2,1,0:T(8,128)S(1)}, u32[]{:S(2)}, u32[]{:S(2)}) %collective-permute-start.1) | collective-permute-done | bytes 245792 | tf_op jit(solution)/shard_map/ppermute | solution.py:27
  69.2 7.4 %collective-permute-done.2 = f32[6,5,16,128]{3,2,1,0:T(8,128)S(1)} collective-permute-done((f32[6,5,16,128]{3,2,1,0:T(8,128)S(1)}, f32[6,5,16,128]{3,2,1,0:T(8,128)S(1)}, u32[]{:S(2)}, u32[]{:S(2)}) %collective-permute-start.2) | collective-permute-done | bytes 245792 | tf_op jit(solution)/shard_map/ppermute | solution.py:28
  85.1 10.0 %add.346 = f32[8,2,8,2,64,2]{5,4,3,2,1,0:T(8,128)} reshape(f32[16,16,128]{2,1,0:T(8,128)S(1)} %get-tuple-element.6) | data formatting | bytes 262144 | tf_op jit(solution)/shard_map/add | solution.py:212
  95.1 4.0 %reduce_sum.57 = f32[8,8,64]{2,1,0:T(8,128)S(1)} reduce(f32[8,2,8,2,64,2]{5,4,3,2,1,0:T(8,128)} %add.346, f32[]{:T(128)} %constant.162.clone.1), dimensions={1,3,5}, to_apply=%region_3.4 | reduce | flops 28672 | bytes 147460 | tf_op jit(solution)/shard_map/reduce_sum | solution.py:169
  99.2 9.7 %reshape.348 = f32[8,2,8,2,64,2]{5,4,3,2,1,0:T(8,128)} reshape(f32[1,16,16,128]{3,2,1,0:T(8,128)S(1)} %get-tuple-element.66) | data formatting | bytes 262144 | tf_op jit(solution)/shard_map/reshape | solution.py:168
  108.9 4.0 %reduce_sum.56 = f32[8,8,64]{2,1,0:T(8,128)S(1)} reduce(f32[8,2,8,2,64,2]{5,4,3,2,1,0:T(8,128)} %reshape.348, f32[]{:T(128)} %constant.162.clone.1), dimensions={1,3,5}, to_apply=%region_2.3 | reduce | flops 28672 | bytes 147460 | tf_op jit(solution)/shard_map/reduce_sum | solution.py:169
  113.0 9.7 %reshape.347 = f32[8,2,8,2,64,2]{5,4,3,2,1,0:T(8,128)} reshape(f32[1,16,16,128]{3,2,1,0:T(8,128)S(1)} %slice.664) | data formatting | bytes 262144 | tf_op jit(solution)/shard_map/reshape | solution.py:168
  122.8 4.0 %reduce_sum.55 = f32[8,8,64]{2,1,0:T(8,128)S(1)} reduce(f32[8,2,8,2,64,2]{5,4,3,2,1,0:T(8,128)} %reshape.347, f32[]{:T(128)} %constant.162.clone.1), dimensions={1,3,5}, to_apply=%region_1.2 | reduce | flops 28672 | bytes 147460 | tf_op jit(solution)/shard_map/reduce_sum | solution.py:169
  126.9 9.7 %add.348 = f32[8,2,8,2,64,2]{5,4,3,2,1,0:T(8,128)} reshape(f32[16,16,128]{2,1,0:T(8,128)S(1)} %get-tuple-element.5) | data formatting | bytes 262144 | tf_op jit(solution)/shard_map/add | solution.py:213
  136.6 4.0 %reduce_sum.58 = f32[8,8,64]{2,1,0:T(8,128)S(1)} reduce(f32[8,2,8,2,64,2]{5,4,3,2,1,0:T(8,128)} %add.348, f32[]{:T(128)} %constant.162.clone.1), dimensions={1,3,5}, to_apply=%region_4.5 | reduce | flops 28672 | bytes 147460 | tf_op jit(solution)/shard_map/reduce_sum | solution.py:169
  143.6 3.5 %all_to_all.20 = f32[2,1,12288]{2,1,0:T(1,128)S(1)} all-to-all(f32[2,1,12288]{2,1,0:T(1,128)S(1)} %reshape.397), channel_id=1, replica_groups=mesh['tm'=32,'space_0'=4,'space_1'=2,'space_2'=2] {'space_2'}, dimensions={0} | all-to-all | bytes 196608 | tf_op jit(solution)/shard_map/all_to_all | solution.py:48
  149.6 8.5 %all-to-all-start.1 = ((f32[8,1,3072]{2,1,0:T(1,128)}), f32[8,1,3072]{2,1,0:T(1,128)S(1)}, u32[]{:S(2)}, u32[]{:S(2)}) async-start(f32[8,1,3072]{2,1,0:T(1,128)} %reshape.399), calls=%async_computation.1 | async-start | bytes 196608 | tf_op jit(solution)/shard_map/all_to_all | solution.py:48
  158.4 13.8 %all-to-all-done.1 = f32[8,1,3072]{2,1,0:T(1,128)S(1)} async-done(((f32[8,1,3072]{2,1,0:T(1,128)}), f32[8,1,3072]{2,1,0:T(1,128)S(1)}, u32[]{:S(2)}, u32[]{:S(2)}) %all-to-all-start.1) | async-done | bytes 98336 | tf_op jit(solution)/shard_map/all_to_all | solution.py:48
  175.3 7.4 %all-to-all-start.2 = ((f32[32,256,32]{1,2,0:T(8,128)}), f32[32,256,32]{1,2,0:T(8,128)S(1)}, u32[]{:S(2)}, u32[]{:S(2)}) async-start(f32[32,256,32]{1,2,0:T(8,128)} %broadcast_in_dim.60), calls=%async_computation.2 | async-start | bytes 2097152 | tf_op jit(solution)/shard_map/all_to_all | solution.py:60
  184.7 48.1 %all-to-all-done.2 = f32[32,256,32]{1,2,0:T(8,128)S(1)} async-done(((f32[32,256,32]{1,2,0:T(8,128)}), f32[32,256,32]{1,2,0:T(8,128)S(1)}, u32[]{:S(2)}, u32[]{:S(2)}) %all-to-all-start.2) | async-done | bytes 1048608 | tf_op jit(solution)/shard_map/all_to_all | solution.py:60
  236.3 7.2 %all-to-all-start.3 = ((f32[16,1,768]{2,1,0:T(1,128)}), f32[16,1,768]{2,1,0:T(1,128)S(1)}, u32[]{:S(2)}, u32[]{:S(2)}) async-start(f32[16,1,768]{2,1,0:T(1,128)} %reshape.401), calls=%async_computation.3 | async-start | bytes 98304 | tf_op jit(solution)/shard_map/all_to_all | solution.py:252
  244.2 13.9 %all-to-all-done.3 = f32[16,1,768]{2,1,0:T(1,128)S(1)} async-done(((f32[16,1,768]{2,1,0:T(1,128)}), f32[16,1,768]{2,1,0:T(1,128)S(1)}, u32[]{:S(2)}, u32[]{:S(2)}) %all-to-all-start.3) | async-done | bytes 49184 | tf_op jit(solution)/shard_map/all_to_all | solution.py:252
  265.0 3.3 %copy.150 = f32[1,5,16,16,128]{4,3,2,1,0:T(8,128)S(1)} copy(f32[1,5,16,16,128]{3,2,4,1,0:T(8,128)} %bitcast.170) | data formatting | bytes 1310720 | tf_op jit(solution)/shard_map/reshape | solution.py:257
  (155 shorter events, 38.7 us)
Async XLA Ops:
  0.9 22.7 %collective-permute-start = (f32[16,16,128]{2,1,0:T(8,128)S(1)}, f32[16,16,128]{2,1,0:T(8,128)S(1)}, u32[]{:S(2)}, u32[]{:S(2)}) collective-permute-start(f32[16,16,128]{2,1,0:T(8,128)S(1)} %slice_bitcast_fusion.2), channel_id=1, source_target_pairs={{0,16},{16,32},{32,48},{48,64},{64,80},{80,96},{96,112},{112,128},... | collective-permute-start | bytes 393224 | tf_op jit(solution)/shard_map/ppermute | solution.py:17
  21.7 2.0 copy-start.2
  24.3 9.7 %copy-start = (f32[1,5,16,16,128]{4,3,2,1,0:T(8,128)S(1)}, f32[1,5,16,16,128]{4,3,2,1,0:T(8,128)}, u32[]{:S(2)}) copy-start(f32[1,5,16,16,128]{4,3,2,1,0:T(8,128)} %param.4) | copy-start | bytes 1966084
  34.1 35.1 %collective-permute-start.1 = (f32[6,5,16,128]{3,2,1,0:T(8,128)S(1)}, f32[6,5,16,128]{3,2,1,0:T(8,128)S(1)}, u32[]{:S(2)}, u32[]{:S(2)}) collective-permute-start(f32[6,5,16,128]{3,2,1,0:T(8,128)S(1)} %get-tuple-element.35), channel_id=1, source_target_pairs={{0,1},{1,2},{2,3},{3,4},{4,5},{5,6},{6,7},{7,8},{8,9},{9,10},{10,1... | collective-permute-start | bytes 737288 | tf_op jit(solution)/shard_map/ppermute | solution.py:27
  49.5 27.1 %collective-permute-start.2 = (f32[6,5,16,128]{3,2,1,0:T(8,128)S(1)}, f32[6,5,16,128]{3,2,1,0:T(8,128)S(1)}, u32[]{:S(2)}, u32[]{:S(2)}) collective-permute-start(f32[6,5,16,128]{3,2,1,0:T(8,128)S(1)} %get-tuple-element.36), channel_id=1, source_target_pairs={{1,0},{2,1},{3,2},{4,3},{5,4},{6,5},{7,6},{8,7},{9,8},{10,9},{11,1... | collective-permute-start | bytes 737288 | tf_op jit(solution)/shard_map/ppermute | solution.py:28
  77.8 0.9 copy-start.3
  149.6 22.6 %all-to-all-start.1 = ((f32[8,1,3072]{2,1,0:T(1,128)}), f32[8,1,3072]{2,1,0:T(1,128)S(1)}, u32[]{:S(2)}, u32[]{:S(2)}) async-start(f32[8,1,3072]{2,1,0:T(1,128)} %reshape.399), calls=%async_computation.1 | async-start | bytes 196608 | tf_op jit(solution)/shard_map/all_to_all | solution.py:48
  175.3 57.5 %all-to-all-start.2 = ((f32[32,256,32]{1,2,0:T(8,128)}), f32[32,256,32]{1,2,0:T(8,128)S(1)}, u32[]{:S(2)}, u32[]{:S(2)}) async-start(f32[32,256,32]{1,2,0:T(8,128)} %broadcast_in_dim.60), calls=%async_computation.2 | async-start | bytes 2097152 | tf_op jit(solution)/shard_map/all_to_all | solution.py:60
  236.3 24.1 %copy-start.4 = (f32[5,3,1,1]{0,1,3,2:T(4,128)S(1)}, f32[5,3,1,1]{0,1,3,2:T(4,128)}, u32[]{:S(2)}) copy-start(f32[5,3,1,1]{0,1,3,2:T(4,128)} %constant.174) | copy-start | bytes 184
  236.3 21.7 %all-to-all-start.3 = ((f32[16,1,768]{2,1,0:T(1,128)}), f32[16,1,768]{2,1,0:T(1,128)S(1)}, u32[]{:S(2)}, u32[]{:S(2)}) async-start(f32[16,1,768]{2,1,0:T(1,128)} %reshape.401), calls=%async_computation.3 | async-start | bytes 98304 | tf_op jit(solution)/shard_map/all_to_all | solution.py:252
  265.0 3.3 %copy-start.1 = (f32[1,5,16,16,128]{4,3,2,1,0:T(8,128)S(1)}, f32[1,5,16,16,128]{4,3,2,1,0:T(8,128)}, u32[]{:S(2)}) copy-start(f32[1,5,16,16,128]{4,3,2,1,0:T(8,128)} %bitcast_dynamic-update-slice_fusion) | copy-start | bytes 1966084
